TPU v7x, 32 devices: a whole 2x2x4 slice. The times are simulated.
32 devices in a mesh: wide: 16 (over z, y, x), narrow: 2 (over core).
Axes of the slice: x: 2, y: 2, z: 4, core: 2. Of those that a mesh axis runs over, the one named last changes fastest.
Arguments:
- points: bfloat16 [32, 1024, 512], P('wide', 'narrow'), may hold values from -6 to 6
- counts: int32 [32, 256], P('wide', 'narrow'), may hold values from 1 to 4, as said below
- destination: int32 [32, 256], P('wide', 'narrow'), may hold values from 0 to 15, as said below
- rotated_ball: int32 [32, 256], P('wide', 'narrow'), may hold values from 0 to 1
- qkv_first: bfloat16 [512, 1536], replicated, may hold values from -1 to 1
- out_first: bfloat16 [512, 512], replicated, may hold values from -0.25 to 0.25
- qkv_second: bfloat16 [512, 1536], replicated, may hold values from -1 to 1
- out_second: bfloat16 [512, 512], replicated, may hold values from -0.25 to 0.25
Outputs:
- result: bfloat16 [32, 1024, 512], P('wide', 'narrow')
Inputs may be any that keep to these rules, and one draw needn't show every extreme that they name: `counts`: the first block of every ball row has all 4 points usable. Among the blocks of one device, at most 32 have the same destination; on every device some destination receives 32 of its blocks, and some destination receives 32 blocks from every device of its narrow index.
All inputs are finite; a program needn't handle non-finite values.
Results may differ from a plain program's by a relative error of at most 0.0095.
Values may be sent and summed in bfloat16 or wider, within the bound.
No kernel may reach another device: no remote copies, remote signals or barrier semaphores. Data moves between devices by JAX's collectives and lax.ppermute only.
A program may use at most 128 MiB of HBM per device.

v0:
```python
import functools
import math

import jax
import jax.numpy as jnp
from jax import lax
from jax.experimental import pallas as pl
from jax.experimental.pallas import tpu as pltpu
from jax.sharding import PartitionSpec as P

HEADS = 8
BLK = 4
EPSILON = 1e-06
NEGATIVE = -1e30
LANES = 128
TILE = 256
VMEM_LIMIT = 56 * 1024 * 1024
BF16 = jnp.bfloat16
F32 = jnp.float32
I32 = jnp.int32

NT = (((1,), (1,)), ((), ()))


def iota(shape, axis):
    return lax.broadcasted_iota(I32, shape, axis)


def mm(left, right):
    return jnp.dot(left, right, preferred_element_type=F32)


def mm_t(left, right):
    return lax.dot_general(left, right, NT, preferred_element_type=F32)


def params():
    return pltpu.CompilerParams(vmem_limit_bytes=VMEM_LIMIT)


def whole(array):
    return pl.BlockSpec(array.shape, lambda *_: (0,) * len(array.shape))


def normalize(rows):
    return (rows * lax.rsqrt(jnp.mean(rows * rows, axis=-1, keepdims=True) + EPSILON)).astype(BF16)


def project_rows(normed, weight, width):
    factor = math.log2(math.e) / math.sqrt(width // HEADS)
    query = (mm(normed, weight[:, :width]) * factor).astype(BF16)
    return query, mm(normed, weight[:, width:]).astype(BF16)


def block_digits(values):
    digits = jnp.concatenate([values // 32, values % 32] + [jnp.zeros_like(values)] * 6, axis=0)
    return digits.astype(F32).astype(BF16)


def point_row(values):
    blocks = values.shape[1]
    spread = iota((blocks, blocks * BLK), 1) // BLK == iota((blocks, blocks * BLK), 0)
    digits = mm(block_digits(values), jnp.where(spread, 1.0, 0.0).astype(BF16)).astype(I32)
    return (digits[:1] * 32 + digits[1:2]) * BLK + iota((1, blocks * BLK), 1) % BLK


def point_column(values):
    blocks = values.shape[1]
    spread = iota((blocks * BLK, blocks), 0) // BLK == iota((blocks * BLK, blocks), 1)
    digits = mm_t(jnp.where(spread, 1.0, 0.0).astype(BF16), block_digits(values)).astype(I32)
    return (digits[:, :1] * 32 + digits[:, 1:2]) * BLK + iota((blocks * BLK, 1), 0) % BLK


def own_half(lane, head):
    return (lane < LANES // 2) if head == 0 else (lane >= LANES // 2)


def softmax_mix(scores, values):
    highest = functools.reduce(jnp.maximum, [jnp.max(s, axis=-1, keepdims=True) for s in scores])
    total = None
    for s, v in zip(scores, values):
        wide = jnp.concatenate([v, jnp.ones_like(v)], axis=1)
        part = mm(jnp.exp2(s - highest).astype(BF16), wide)
        total = part if total is None else total + part
    return total[:, :LANES] / total[:, LANES:]


def first_projection_kernel(
    width, points_ref, counts_ref, weight_ref, query_ref, kv_ref, pooled_ref, bias_ref
):
    normed = normalize(points_ref[0].astype(F32))
    query, kv = project_rows(normed, weight_ref, width)
    query_ref[0] = query
    kv_ref[0] = kv
    share = normed.shape[0]
    blocks = share // BLK
    block = iota((blocks, share), 0)
    point = iota((blocks, share), 1)
    own = point // BLK == block
    counts = jnp.broadcast_to(counts_ref[0], (8, blocks)).astype(F32).astype(BF16)
    fill = mm(counts, jnp.where(own, 1.0, 0.0).astype(BF16))[:1].astype(I32)
    usable = point[:1] % BLK < fill
    bias_ref[0] = jnp.where(usable, 0.0, NEGATIVE)
    chosen = jnp.where(own & usable, 1.0, 0.0)
    count = jnp.sum(chosen, axis=1, keepdims=True)
    pooled_ref[0] = (mm(chosen.astype(BF16), kv) / count).astype(BF16)


def first_projection(points, counts, weight):
    balls, share, width = points.shape
    blocks = share // BLK
    ball = lambda rows, cols: pl.BlockSpec((1, rows, cols), lambda b: (b, 0, 0))
    return pl.pallas_call(
        functools.partial(first_projection_kernel, width),
        grid=(balls,),
        in_specs=[ball(share, width), ball(1, blocks), whole(weight)],
        out_specs=[
            ball(share, width), ball(share, 2 * width), ball(blocks, 2 * width), ball(1, share),
        ],
        out_shape=[
            jax.ShapeDtypeStruct((balls, share, width), BF16),
            jax.ShapeDtypeStruct((balls, share, 2 * width), BF16),
            jax.ShapeDtypeStruct((balls, blocks, 2 * width), BF16),
            jax.ShapeDtypeStruct((balls, 1, share), F32),
        ],
        compiler_params=params(),
        cost_estimate=pl.CostEstimate(
            flops=2 * balls * share * width * 3 * width, bytes_accessed=8 * balls * share * width,
            transcendentals=0,
        ),
        name="first_projection",
    )(points, counts.reshape(balls, 1, blocks), weight)


def joined(parts):
    return parts[0] if len(parts) == 1 else jnp.concatenate(parts, axis=0)


def first_attention_kernel(
    width, shares, query_ref, kv_ref, bias_ref, points_ref, out_ref, *refs
):
    coarse_refs = refs[:shares]
    layer_ref, normed_ref, attended = refs[-3:]
    share = points_ref.shape[1]
    tile = min(2 * TILE, share)
    bias = bias_ref[0]

    def one_pair(pair, carry):
        at = pl.multiple_of(pair * LANES, LANES)
        value_at = pl.multiple_of(width + pair * LANES, LANES)
        keys, values = kv_ref[0, :, pl.ds(at, LANES)], kv_ref[0, :, pl.ds(value_at, LANES)]
        coarse_keys = joined([ref[0, :, pl.ds(at, LANES)] for ref in coarse_refs])
        coarse_values = joined([ref[0, :, pl.ds(value_at, LANES)] for ref in coarse_refs])
        for row in range(0, share, tile):
            query = query_ref[0, pl.ds(row, tile), pl.ds(at, LANES)]
            lane = iota(query.shape, 1)
            results = []
            for head in range(2):
                own = own_half(lane, head)
                q = jnp.where(own, query, jnp.zeros_like(query))
                results.append(
                    softmax_mix(
                        [mm_t(q, keys) + bias, mm_t(q, coarse_keys)], [values, coarse_values]
                    )
                )
            mixture = jnp.where(own_half(lane, 0), results[0], results[1])
            attended[pl.ds(row, tile), pl.ds(at, LANES)] = mixture.astype(BF16)
        return carry

    lax.fori_loop(0, width // LANES, one_pair, 0, unroll=4)
    layer = points_ref[0].astype(F32) + mm(attended[...], out_ref[...])
    layer = layer.astype(BF16)
    layer_ref[0] = layer
    normed_ref[0] = normalize(layer.astype(F32))


def first_attention(index, query, kv, coarse, bias, points, weight, earlier):
    balls, share, width = points.shape
    coarse_rows = sum(part.shape[1] for part in coarse)
    ball = lambda rows, cols: pl.BlockSpec((1, rows, cols), lambda _: (index, 0, 0))
    return pl.pallas_call(
        functools.partial(first_attention_kernel, width, len(coarse)),
        grid=(1,),
        in_specs=[
            ball(share, width), ball(share, 2 * width), ball(1, share), ball(share, width),
            whole(weight),
        ] + [ball(part.shape[1], 2 * width) for part in coarse]
        + [pl.BlockSpec(memory_space=pl.ANY)] * len(earlier),
        out_specs=[ball(share, width), ball(share, width)],
        out_shape=[jax.ShapeDtypeStruct((balls, share, width), BF16)] * 2,
        input_output_aliases={5 + len(coarse) + i: i for i in range(len(earlier))},
        scratch_shapes=[pltpu.VMEM((share, width), BF16)],
        compiler_params=params(),
        cost_estimate=pl.CostEstimate(
            flops=16 * share * (share + coarse_rows) * width,
            bytes_accessed=16 * share * width,
            transcendentals=HEADS * share * (share + coarse_rows),
        ),
        name="first_attention",
    )(query, kv, bias, points, weight, *coarse, *earlier)


def pack_kernel(route_index, offset, slots_ref, rows_ref, packed_ref):
    step = packed_ref.shape[0]
    target = offset + pl.program_id(0) * step + iota((step, rows_ref.shape[0]), 0)
    slot = point_row(slots_ref[route_index : route_index + 1, :])
    chosen = jnp.where(target == slot, 1.0, 0.0).astype(BF16)
    packed_ref[...] = mm(chosen, rows_ref[...]).astype(BF16)


def pack(slots, route_index, rows, packed_rows, offset=0):
    count, width = rows.shape
    step = min(2 * TILE, packed_rows)
    return pl.pallas_call(
        functools.partial(pack_kernel, route_index, offset),
        grid=(packed_rows // step,),
        in_specs=[whole(slots), whole(rows)],
        out_specs=pl.BlockSpec((step, width), lambda t: (t, 0)),
        out_shape=jax.ShapeDtypeStruct((packed_rows, width), BF16),
        compiler_params=params(),
        cost_estimate=pl.CostEstimate(
            flops=2 * packed_rows * width * count, bytes_accessed=4 * packed_rows * width,
            transcendentals=0,
        ),
        name="pack",
    )(slots, rows)


def pack_beside_kernel(here_ref, slots_ref, rows_ref, taken_ref, out_ref):
    units, _, rows, width = out_ref.shape
    slot = point_row(slots_ref[0:1, :])
    chosen = jnp.where(iota((units * rows, rows_ref.shape[0]), 0) == slot, 1.0, 0.0).astype(BF16)
    packed = mm(chosen, rows_ref[...]).astype(BF16)
    core = here_ref[0]
    out_ref[:, pl.ds(core, 1)] = packed.reshape(units, 1, rows, width)
    out_ref[:, pl.ds(1 - core, 1)] = taken_ref[...].reshape(units, 1, rows, width)


def pack_beside(here, slots, rows, taken, units):
    half, width = taken.shape
    shape = (units, 2, half // units, width)
    out = pl.pallas_call(
        pack_beside_kernel,
        grid=(1,),
        in_specs=[
            pl.BlockSpec(memory_space=pltpu.SMEM), whole(slots), whole(rows), whole(taken),
        ],
        out_specs=pl.BlockSpec(shape, lambda _: (0, 0, 0, 0)),
        out_shape=jax.ShapeDtypeStruct(shape, BF16),
        compiler_params=params(),
        cost_estimate=pl.CostEstimate(
            flops=2 * half * width * rows.shape[0], bytes_accessed=8 * half * width,
            transcendentals=0,
        ),
        name="pack_beside",
    )(here, slots, rows, taken)
    return out.reshape(2 * half, width)


def arrange_kernel(factor, limits_ref, rows_ref, place_ref, weight_ref, out_ref):
    tile, width = out_ref.shape
    first = pl.program_id(0) * tile

    @pl.when(first < limits_ref[0, 2])
    def _():
        target = first + iota((tile, rows_ref.shape[0]), 0)
        chosen = jnp.where(target == point_row(place_ref[...]), 1.0, 0.0).astype(BF16)
        normed = mm(chosen, rows_ref[...]).astype(BF16)
        out_ref[...] = (mm(normed, weight_ref[...]) * factor).astype(BF16)

    @pl.when(first >= limits_ref[0, 2])
    def _():
        out_ref[...] = jnp.zeros_like(out_ref)


def arrange(places, rows, weight):
    place, _, limits, _ = places
    count, width = rows.shape
    factor = math.log2(math.e) / math.sqrt(width // HEADS)
    tile = min(2 * TILE, count)
    return pl.pallas_call(
        functools.partial(arrange_kernel, factor),
        grid=(count // tile,),
        in_specs=[
            pl.BlockSpec(memory_space=pltpu.SMEM), whole(rows), whole(place),
            pl.BlockSpec((width, width), lambda t: (0, 0)),
        ],
        out_specs=pl.BlockSpec((tile, width), lambda t: (t, 0)),
        out_shape=jax.ShapeDtypeStruct((count, width), BF16),
        compiler_params=params(),
        cost_estimate=pl.CostEstimate(
            flops=2 * count * width * (count + width), bytes_accessed=4 * count * width,
            transcendentals=0,
        ),
        name="arrange",
    )(limits, rows, place, weight)


def rotated_attention_kernel(
    parts, step, tile, eager, limits_ref, bounds_ref, place_ref, query_ref, key_weight_ref,
    value_weight_ref, *refs
):
    rows_refs, key_places = refs[:parts], refs[parts : 2 * parts]
    mixture_ref, attended, marked, values_all, column = refs[2 * parts :]
    query_rows, width = query_ref.shape
    key_rows = values_all.shape[0]
    pairs = width // LANES
    portion = min(2 * tile, key_rows)

    def inside(rows, first, which):
        row = first + iota((rows, LANES), 0)
        return (row >= bounds_ref[which : which + 1, :]) & (row < bounds_ref[which + 1 : which + 2, :])

    def mark(first, keys):
        span = pl.ds(first, portion)
        closed = jnp.where(inside(portion, first, 2), 0.0, NEGATIVE).astype(BF16)
        lane = iota((portion, LANES), 1)
        for pair in range(pairs):
            at = slice(pair * LANES, (pair + 1) * LANES)
            for head in range(2):
                marked[head, span, at] = jnp.where(own_half(lane, head), keys[:, at], closed)

    def no_keys(index, carry):
        first = pl.multiple_of(index * portion, portion)
        values_all[pl.ds(first, portion), :] = jnp.zeros((portion, width), BF16)
        mark(first, jnp.zeros((portion, width), BF16))
        return carry

    def make_keys(index, carry):
        first = pl.multiple_of(index * portion, portion)
        normed = None
        for rows_ref, key_place in zip(rows_refs, key_places):
            target = first + iota((portion, key_place.shape[1]), 0)
            chosen = jnp.where(target == key_place[...], 1.0, 0.0).astype(BF16)
            part = mm(chosen, rows_ref[...])
            normed = part if normed is None else normed + part
        normed = normed.astype(BF16)
        keys = mm(normed, key_weight_ref[...]).astype(BF16)
        values_all[pl.ds(first, portion), :] = mm(normed, value_weight_ref[...]).astype(BF16)
        mark(first, keys)
        return carry

    live = (limits_ref[0, 3] + portion - 1) // portion
    lax.fori_loop(0, live, make_keys, 0)
    lax.fori_loop(live, key_rows // portion, no_keys, 0)

    def attend(index, first_key, keys, pair):
        lanes = pl.ds(pl.multiple_of(pair * LANES, LANES), LANES)
        rows = pl.ds(pl.multiple_of(index * step, step), step)
        span = pl.ds(pl.multiple_of(first_key, tile), keys)
        query = query_ref[rows, lanes]
        values = values_all[span, lanes]
        label = jnp.where(inside(step, index * step, 0), 1.0, 0.0).astype(BF16)
        lane = iota(query.shape, 1)
        results = []
        for head in range(2):
            q = jnp.where(own_half(lane, head), query, label)
            results.append(softmax_mix([mm_t(q, marked[head, span, lanes])], [values]))
        mixture = jnp.where(own_half(lane, 0), results[0], results[1])
        attended[rows, lanes] = mixture.astype(BF16)

    def one_query_tile(index, carry):
        first_tile, tiles = limits_ref[index, 0], limits_ref[index, 1]

        @pl.when(tiles == 0)
        def _():
            rows = pl.ds(pl.multiple_of(index * step, step), step)
            attended[rows, :] = jnp.zeros((step, attended.shape[1]), BF16)

        all_tiles = key_rows // tile
        fewer = 0
        for count in sorted({min(count, all_tiles) for count in (1, 2, 3, 4, 6, 8, all_tiles)}):

            @pl.when((tiles > fewer) & (tiles <= count))
            def _(count=count):
                together = math.gcd(pairs, 4 if 2 * count <= eager else 2 if count <= eager else 1)
                first_key = jnp.minimum(first_tile, all_tiles - count) * tile

                def some_pairs(step, inner):
                    for pair in range(together):
                        attend(index, first_key, count * tile, step * together + pair)
                    return inner

                lax.fori_loop(0, pairs // together, some_pairs, 0)

            fewer = count
        return carry

    lax.fori_loop(0, query_rows // step, one_query_tile, 0)

    def one_tile(index, carry):
        at = pl.multiple_of(index * step, step)
        place = column[pl.ds(at, step), :]
        chosen = jnp.where(iota((step, query_rows), 1) == place, 1.0, 0.0).astype(BF16)
        mixture_ref[pl.ds(at, step), :] = mm(chosen, attended[...]).astype(BF16)
        return carry

    column[...] = point_column(place_ref[...])
    lax.fori_loop(0, query_rows // step, one_tile, 0)


def rotated_attention(places, query, parts, weight, key_rows, eager):
    place, key_places, limits, bounds = places
    rows, width = query.shape
    step, tile = query_step(rows), min(TILE, rows)
    return pl.pallas_call(
        functools.partial(rotated_attention_kernel, len(parts), step, tile, eager),
        grid=(1,),
        in_specs=[
            pl.BlockSpec(memory_space=pltpu.SMEM), whole(bounds), whole(place), whole(query),
            pl.BlockSpec((width, width), lambda _: (0, 1)), pl.BlockSpec((width, width), lambda _: (0, 2)),
        ] + [whole(array) for array in list(parts) + list(key_places)],
        out_specs=pl.BlockSpec((rows, width), lambda _: (0, 0)),
        out_shape=jax.ShapeDtypeStruct((rows, width), BF16),
        scratch_shapes=[
            pltpu.VMEM((rows, width), BF16), pltpu.VMEM((2, key_rows, width), BF16),
            pltpu.VMEM((key_rows, width), BF16), pltpu.VMEM((rows, 1), I32),
        ],
        compiler_params=params(),
        cost_estimate=pl.CostEstimate(
            flops=8 * rows * key_rows * width, bytes_accessed=10 * rows * width,
            transcendentals=rows * key_rows * HEADS // 2,
        ),
        name="rotated_attention",
    )(limits, bounds, place, query, weight, weight, *parts, *key_places)


def finish_kernel(route_index, slots_ref, layer_ref, weight_ref, *refs):
    returned, result_ref, all_slots = refs[:-2], refs[-2], refs[-1]
    share = layer_ref.shape[1]

    @pl.when(pl.program_id(0) == 0)
    def _():
        all_slots[...] = point_column(slots_ref[route_index : route_index + 1, :])

    slot = all_slots[pl.ds(pl.multiple_of(pl.program_id(0) * share, share), share), :]
    attended, first = None, 0
    for part in returned:
        target = first + iota((share, part.shape[0]), 1)
        found = mm(jnp.where(target == slot, 1.0, 0.0).astype(BF16), part[...])
        attended = found if attended is None else attended + found
        first += part.shape[0]
    layer = layer_ref[0].astype(F32)
    result_ref[0] = (layer + mm(attended.astype(BF16), weight_ref[...])).astype(BF16)


def finish(slots, route_index, layer, weight, returned):
    balls, share, width = layer.shape
    ball = lambda rows, cols: pl.BlockSpec((1, rows, cols), lambda b: (b, 0, 0))
    rows = sum(part.shape[0] for part in returned)
    return pl.pallas_call(
        functools.partial(finish_kernel, route_index),
        grid=(balls,),
        in_specs=[whole(slots), ball(share, width), whole(weight)]
        + [whole(part) for part in returned],
        out_specs=ball(share, width),
        out_shape=jax.ShapeDtypeStruct(layer.shape, BF16),
        scratch_shapes=[pltpu.VMEM((balls * share, 1), I32)],
        compiler_params=params(),
        cost_estimate=pl.CostEstimate(
            flops=2 * balls * share * width * (rows + width),
            bytes_accessed=8 * balls * share * width, transcendentals=0,
        ),
        name="finish",
    )(slots, layer, weight, *returned)


def side_by_side(mine, other, lower, axis):
    return jnp.where(
        lower, jnp.concatenate([mine, other], axis=axis), jnp.concatenate([other, mine], axis=axis)
    )


def double(array, axis_name, step, axis):
    count = lax.axis_size(axis_name)
    other = lax.ppermute(array, axis_name, [(i, i ^ step) for i in range(count)])
    return side_by_side(array, other, (lax.axis_index(axis_name) & step) == 0, axis)


def gather_shares(array, axis_name, axis):
    count = lax.axis_size(axis_name)
    if count & (count - 1):
        return lax.all_gather(array, axis_name, axis=axis, tiled=True)
    step = 1
    while step < count:
        array = double(array, axis_name, step, axis)
        step *= 2
    return array


def exchange(rows, wide_count):
    parts = rows.reshape((wide_count, rows.shape[0] // wide_count) + rows.shape[1:])
    parts = lax.all_to_all(parts, "wide", split_axis=0, concat_axis=0, tiled=True)
    return parts.reshape(rows.shape)


def earlier_sum(values):
    return jnp.cumsum(values, axis=-1, dtype=I32) - values


def query_step(rows):
    return min(TILE, rows)


def sorted_places(label, fill, own_blocks, labels, key_parts, tile):
    member = (label[None, :] == jnp.arange(labels, dtype=I32)[:, None]).astype(I32)
    own = member[:, :own_blocks]
    own_total = jnp.sum(own, axis=1, dtype=I32)
    own_start = earlier_sum(own_total)
    own_end = own_start + own_total
    query_at = jnp.sum(own * (own_start[:, None] + earlier_sum(own)), axis=0, dtype=I32)
    nowhere = 2 * own_blocks
    query_place = jnp.where(label[:own_blocks] >= 0, query_at, nowhere).reshape(1, -1)
    usable = member * fill[None, :]
    key_total = jnp.sum(usable, axis=1, dtype=I32)
    padded = (key_total + tile - 1) // tile * tile
    room = jnp.sum(padded) <= label.shape[0] * BLK
    key_start = earlier_sum(jnp.where(room, padded, key_total))
    key_end = key_start + key_total
    key_at = jnp.sum(member * (key_start[:, None] + earlier_sum(usable)), axis=0, dtype=I32)
    point = jnp.arange(BLK, dtype=I32)[None, :]
    key_place = jnp.where(point < fill[:, None], key_at[:, None] + point, -1).reshape(-1)
    step = query_step(own_blocks * BLK)
    tiles = own_blocks * BLK // step
    first = jnp.arange(tiles, dtype=I32)[:, None] * step
    meets = (own_start[None, :] * BLK < first + step) & (own_end[None, :] * BLK > first)
    meets = meets & (own_total[None, :] > 0)
    low = jnp.min(jnp.where(meets, key_start[None, :], label.shape[0] * BLK), axis=1)
    high = jnp.max(jnp.where(meets, key_end[None, :], 0), axis=1)
    low_tile = low // tile
    count = jnp.where(high > 0, (high + tile - 1) // tile - low_tile, 0)
    live = (jnp.sum(own_total) * BLK, jnp.max(key_end))
    live = [jnp.broadcast_to(number, count.shape) for number in live]
    limits = jnp.stack([jnp.where(high > 0, low_tile, 0), count] + live, axis=1)
    bounds = jnp.stack([own_start * BLK, own_end * BLK, key_start, key_end])
    bounds = jnp.pad(bounds, ((0, 4), (0, LANES // 2 - labels)))
    bounds = jnp.concatenate([bounds, bounds], axis=1)
    key_places = [part.reshape(1, -1) for part in jnp.split(key_place, key_parts)]
    return query_place, key_places, limits, bounds


def labels_at(position, values, count):
    at = position[:, None, :] == jnp.arange(count, dtype=I32)[None, :, None]
    return jnp.sum(jnp.where(at, values[:, None, :], 0), axis=-1, dtype=I32)


def by_slots(normed, slots_of, route_index, codes, index, capacity, weight):
    wide_count = codes.shape[0]
    slots = wide_count * capacity
    packed, codes = lax.optimization_barrier((pack(slots_of, route_index, normed, slots * BLK), codes))
    arrived = exchange(packed, wide_count)
    mine = (codes // (2 * BLK)) == index
    rank = jnp.where(mine, earlier_sum(mine.astype(I32)), -1)
    found = labels_at(rank, codes % (2 * BLK) + 1, capacity).reshape(slots)
    live = found > 0
    label = jnp.where(live, (found - 1) // BLK, -1)
    fill = jnp.where(live, (found - 1) % BLK + 1, 0)
    places = sorted_places(label, fill, slots, 2, 1, min(TILE, slots * BLK))
    query = arrange(places, arrived, weight)
    mixture = rotated_attention(places, query, [arrived], weight, arrived.shape[0], 4)
    return [exchange(mixture, wide_count)]


def lower_mask(size):
    return jnp.where(iota((size, size), 0) < iota((size, size), 1), 1.0, 0.0).astype(BF16)


def ones_where(condition):
    return jnp.where(condition, 1.0, 0.0).astype(BF16)


def to_row(column):
    size = column.shape[0]
    same = iota((size, size), 0) == iota((size, size), 1)
    return jnp.sum(jnp.where(same, column, 0.0), axis=0, keepdims=True)


def route_kernel(
    wide_count, capacity, unit, here_ref, codes_ref, starts_ref, slots_ref, straddle_ref
):
    block_count = codes_ref.shape[1]
    lane = iota((1, LANES), 1)
    destination = codes_ref[...] // (2 * BLK)
    worst = jnp.zeros((1, LANES), F32)
    for side in range(2):
        part = destination[side * wide_count : (side + 1) * wide_count]
        held = jnp.zeros((wide_count, LANES), F32)
        for d in range(wide_count):
            count = jnp.sum(jnp.where(part == d, 1.0, 0.0), axis=1, keepdims=True)
            held = jnp.where(lane == d, count, held)
        load = jnp.sum(held, axis=0, keepdims=True)
        starts = jnp.zeros((wide_count, LANES), F32)
        for d in range(wide_count):
            other = load[:, d : d + 1]
            earlier = (other > load) | ((other == load) & (d < lane))
            starts = starts + jnp.where(earlier, held[:, d : d + 1], 0.0)
        starts_ref[pl.ds(side * wide_count, wide_count), :] = starts
        run = jnp.floor(starts * (1.0 / unit))
        last = jnp.floor((starts + held - 1.0) * (1.0 / unit))
        low = jnp.min(jnp.where(held > 0.0, run, 1e6), axis=0, keepdims=True)
        high = jnp.max(jnp.where(held > 0.0, last, -1.0), axis=0, keepdims=True)
        worst = jnp.maximum(worst, jnp.where((high > low) & (lane < wide_count), 1.0, 0.0))
    straddle_ref[0, 0] = jnp.max(worst).astype(I32)

    core = here_ref[0]
    index = core * wide_count + here_ref[1]
    own = codes_ref[pl.ds(index, 1), :] // (2 * BLK)
    start = starts_ref[pl.ds(index, 1), :]
    member = own == iota((wide_count, block_count), 0)
    rank = mm(ones_where(member), lower_mask(block_count))
    rank = jnp.sum(jnp.where(member, rank, 0.0), axis=0, keepdims=True)
    place = rank
    for d in range(wide_count):
        place = place + jnp.where(own == d, start[:, d : d + 1], 0.0)
    place = place.astype(I32)
    run, within = place // unit, place % unit
    half = unit // 2
    away = (within // half != core).astype(I32)
    slots_ref[0:1, :] = away * (block_count // 2) + run * half + within % half
    slots_ref[1:2, :] = own * capacity + rank.astype(I32)


def route(codes, here, wide_count, capacity, unit):
    devices, block_count = codes.shape
    full = lambda shape: pl.BlockSpec(shape, lambda _: (0, 0))
    return pl.pallas_call(
        functools.partial(route_kernel, wide_count, capacity, unit),
        grid=(1,),
        in_specs=[pl.BlockSpec(memory_space=pltpu.SMEM), whole(codes)],
        out_specs=[
            full((devices, LANES)), full((8, block_count)), pl.BlockSpec(memory_space=pltpu.SMEM),
        ],
        out_shape=[
            jax.ShapeDtypeStruct((devices, LANES), F32),
            jax.ShapeDtypeStruct((8, block_count), I32),
            jax.ShapeDtypeStruct((1, 1), I32),
        ],
        compiler_params=params(),
        name="route",
    )(here, codes)


def plan_kernel(
    unit, tile, here_ref, codes_ref, starts_ref,
    query_ref, limits_ref, bounds_ref, *key_refs
):
    wide_count, block_count = codes_ref.shape[0] // 2, codes_ref.shape[1]
    half = unit // 2
    blocks = wide_count * half
    core, side, base = here_ref[0], here_ref[1] % 2, here_ref[1] // 2 * unit
    mine = pl.ds(pl.multiple_of(side * wide_count, wide_count), wide_count)
    codes = codes_ref[mine, :]
    destination = codes // (2 * BLK)
    members = jnp.concatenate([ones_where(destination == d) for d in range(wide_count)], axis=0)
    rank = mm(members, lower_mask(block_count))
    starts = starts_ref[mine, :]
    position = jnp.zeros(codes.shape, F32)
    for d in range(wide_count):
        at = starts[:, d : d + 1] + rank[d * wide_count : (d + 1) * wide_count]
        position = position + jnp.where(destination == d, at, 0.0)
    position = position.astype(I32) - base
    values = codes.astype(F32) + 1.0

    def labels_of(which):
        columns = []
        for source in range(wide_count):
            at = iota((half, block_count), 0) + which * half == position[source : source + 1]
            found = jnp.where(at, values[source : source + 1], 0.0)
            columns.append(jnp.sum(found, axis=1, keepdims=True))
        found = to_row(jnp.concatenate(columns, axis=0)).astype(I32) + (BLK - 1)
        member = found // BLK - 1 == iota((LANES, blocks), 0) % (LANES // 2)
        return member, jnp.where(member, (found % BLK + 1).astype(F32), 0.0)

    earlier = lower_mask(blocks)
    below = iota((LANES, LANES), 1) < iota((LANES, LANES), 0) % (LANES // 2)

    def begin(total):
        return jnp.sum(jnp.where(below, to_row(total), 0.0), axis=1, keepdims=True)

    def place_of(member, at):
        once = member & (iota(member.shape, 0) < LANES // 2)
        return jnp.sum(jnp.where(once, at, 0.0), axis=0, keepdims=True).astype(I32)

    parts = [labels_of(which) for which in (core, 1 - core)]
    own = parts[0][0]
    own_ones = ones_where(own)
    own_total = jnp.sum(jnp.where(own, 1.0, 0.0), axis=1, keepdims=True)
    own_start = begin(own_total)
    query = place_of(own, own_start + mm(own_ones, earlier))
    query_ref[...] = query

    totals = [jnp.sum(fill, axis=1, keepdims=True) for _, fill in parts]
    total = sum(totals)
    padded = jnp.floor((total + (tile - 1)) * (1.0 / tile)) * tile
    once = iota((LANES, 1), 0) < LANES // 2
    room = jnp.sum(jnp.where(once, padded, 0.0), axis=0, keepdims=True) <= 2 * blocks * BLK
    key_start = begin(jnp.where(room, padded, total))
    key_end = key_start + total
    spread = ones_where(iota((blocks, blocks * BLK), 1) // BLK == iota((blocks, blocks * BLK), 0))
    point = iota((1, blocks * BLK), 1) % BLK
    begins = key_start
    for ref, (member, fill), part_total in zip(key_refs, parts, totals):
        at = place_of(member, begins + mm(fill.astype(BF16), earlier))
        count = place_of(member, fill)
        digits = jnp.concatenate([at // 32, at % 32, count] + [jnp.zeros_like(at)] * 5, axis=0)
        digits = mm(digits.astype(F32).astype(BF16), spread).astype(I32)
        ref[...] = jnp.where(point < digits[2:3], digits[:1] * 32 + digits[1:2] + point, -1)
        begins = begins + part_total

    rows = [to_row(c) for c in (own_start * BLK, (own_start + own_total) * BLK, key_start, key_end)]
    bounds_ref[...] = jnp.concatenate(rows + [jnp.zeros_like(rows[0])] * 4, axis=0).astype(I32)
    step = query_step(blocks * BLK)
    first = (iota((8, LANES), 0) * step).astype(F32)
    meets = (rows[0] < first + step) & (rows[1] > first) & (rows[1] > rows[0])
    low = jnp.min(jnp.where(meets, rows[2], 1e6), axis=1, keepdims=True).astype(I32)
    high = jnp.max(jnp.where(meets, rows[3], 0.0), axis=1, keepdims=True).astype(I32)
    low_tile = low // tile
    count = (high + tile - 1) // tile - low_tile
    live = jnp.max(rows[3], axis=1, keepdims=True).astype(I32)
    lane = iota((8, LANES), 1)
    limits = jnp.where(lane == 0, low_tile, jnp.where(lane == 1, count, 0))
    limits = jnp.where(lane == 2, blocks * BLK, jnp.where(lane == 3, live, limits))
    limits_ref[...] = jnp.where((lane < 2) & (high <= 0), 0, limits)


def plan(here, codes, starts, unit, tile):
    wide_count = codes.shape[0] // 2
    rows = wide_count * unit // 2 * BLK
    shapes = [(1, rows // BLK), (8, LANES), (8, LANES)] + [(1, rows)] * 2
    full = lambda shape: pl.BlockSpec(shape, lambda _: (0, 0))
    outs = pl.pallas_call(
        functools.partial(plan_kernel, unit, tile),
        grid=(1,),
        in_specs=[pl.BlockSpec(memory_space=pltpu.SMEM), whole(codes), whole(starts)],
        out_specs=[full(shape) for shape in shapes],
        out_shape=[jax.ShapeDtypeStruct(shape, I32) for shape in shapes],
        compiler_params=params(),
        cost_estimate=pl.CostEstimate(flops=1 << 33, bytes_accessed=1 << 22, transcendentals=0),
        name="plan",
    )(here, codes, starts)
    return outs[0], outs[3:], outs[1], outs[2]


def by_chips(normed, slots, here, codes, starts, weight):
    wide_count, block_count = codes.shape[0] // 2, codes.shape[1]
    unit = 2 * block_count // wide_count
    units = wide_count // 2
    rows_half = block_count * BLK // 2
    swap = lambda array: lax.ppermute(array, "narrow", [(0, 1), (1, 0)])
    is_first = lax.axis_index("narrow") == 0

    def take_apart(array):
        both = array.reshape(units, 2, rows_half // units, -1)
        low, high = both[:, 0].reshape(rows_half, -1), both[:, 1].reshape(rows_half, -1)
        return jnp.where(is_first, low, high), jnp.where(is_first, high, low)

    taken = swap(pack(slots, 0, normed, rows_half, rows_half))
    arrived = exchange(pack_beside(here, slots, normed, taken, units), wide_count)
    tile = min(TILE, 2 * rows_half)
    places = plan(here, codes, starts, unit, tile)
    arrived, places = lax.optimization_barrier((arrived, places))
    partner = swap(arrived)
    query = arrange(places, arrived, weight)
    key_rows = 4 * rows_half

    mixture = rotated_attention(places, query, [arrived, partner], weight, key_rows, 6)
    kept, given = take_apart(exchange(mixture, wide_count))
    return [kept, swap(given)]


def on_device(
    points, counts, destination, rotated_ball, qkv_first, out_first, qkv_second, out_second
):
    balls, share, width = points.shape
    wide_count, narrow_count = lax.axis_size("wide"), lax.axis_size("narrow")
    block_count = destination.size
    capacity = max(2, 2 * block_count // wide_count)

    flat = (block_count,)
    dest_flat = destination.reshape(flat)
    code = (dest_flat * 2 + rotated_ball.reshape(flat)) * BLK + counts.reshape(flat) - 1
    power = not wide_count & (wide_count - 1)
    paired = narrow_count == 2 and power and wide_count > 1 and 2 * wide_count <= LANES // 2
    paired = paired and block_count % wide_count == 0 and capacity * wide_count == 2 * block_count
    paired = paired and TILE <= block_count * BLK <= 8 * TILE and block_count % TILE == 0

    codes = code.reshape(1, 1, block_count)
    if paired:
        cores = [(0, 1), (1, 0)]
        chips = [(i, i ^ 1) for i in range(wide_count)]
        both = [(i, i ^ 3) for i in range(2 * wide_count)]
        mine = (codes, lax.ppermute(codes, "narrow", cores))
        theirs = (
            lax.ppermute(codes, "wide", chips), lax.ppermute(codes, ("wide", "narrow"), both)
        )
        lower = lax.axis_index("narrow") == 0
        codes = side_by_side(
            side_by_side(*mine, lower, 0), side_by_side(*theirs, lower, 0),
            (lax.axis_index("wide") & 1) == 0, 1,
        )
    elif power:
        codes = double(codes, "wide", 1, 1)
    query, kv, pooled, bias = first_projection(points, counts, qkv_first)
    if narrow_count == 2:
        coarse = [pooled, lax.ppermute(pooled, "narrow", [(0, 1), (1, 0)])]
    else:
        coarse = [gather_shares(pooled, "narrow", 1)]
    results = ()
    step = 2
    if power and step < wide_count:
        codes = double(codes, "wide", step, 1)
        step *= 2
    for ball in range(balls):
        if power:
            while step < wide_count and (step < 8 << ball or ball == balls - 1):
                coarse, codes = lax.optimization_barrier((coarse, codes))
                codes = double(codes, "wide", step, 1)
                step *= 2
        results = first_attention(ball, query, kv, coarse, bias, points, out_first, results)
    if not power:
        codes = gather_shares(codes, "wide", 1)
    layer_one, normed = results
    normed = normed.reshape(balls * share, width)

    def slot_route(codes, slots, route_index):
        index = lax.axis_index("wide")
        returned = by_slots(normed, slots, route_index, codes, index, capacity, qkv_second)
        return finish(slots, route_index, layer_one, out_second, returned)

    if not paired:
        onehot = (jnp.arange(wide_count, dtype=I32)[:, None] == dest_flat[None, :]).astype(I32)
        rank = jnp.sum(earlier_sum(onehot) * onehot, axis=0, dtype=I32)
        return slot_route(codes[0], (dest_flat * capacity + rank).reshape(1, -1), 0)

    core = lax.axis_index("narrow")
    here = jnp.stack([core, lax.axis_index("wide")]).astype(I32)
    unit = 2 * block_count // wide_count
    codes = codes.reshape(2 * wide_count, block_count)
    starts, slots, straddle = route(codes, here, wide_count, capacity, unit)
    def chip_route():
        returned = by_chips(normed, slots, here, codes, starts, qkv_second)
        return finish(slots, 0, layer_one, out_second, returned)

    def own_labels():
        return codes.reshape(2, wide_count, block_count)[core]

    return lax.cond(
        straddle[0, 0] == 0, chip_route, lambda: slot_route(own_labels(), slots, 1)
    )


def solution(mesh):
    split = P("wide", "narrow")
    in_specs = (P("wide", "narrow", None), split, split, split, P(), P(), P(), P())
    out_specs = P("wide", "narrow", None)
    return jax.shard_map(
        on_device, mesh=mesh, in_specs=in_specs, out_specs=out_specs, check_vma=False
    )
```

profile of v0, /device:TPU:9, one launch (start us, length us, event | category | flops | bytes accessed | tf_op | source)
XLA Modules:
  0.0 139.5 jit_solution(14224189529864056423)
XLA Ops:
  0.0 0.7 add_add_fusion.1
  0.7 1.2 collective-permute-start.5
  1.9 1.0 collective-permute-start.4
  2.9 0.1 collective-permute-start.6
  3.0 5.2 %first_projection.1 = (bf16[2,512,512]{2,1,0:T(8,128)(2,1)}, bf16[2,512,1024]{2,1,0:T(8,128)(2,1)}, bf16[2,128,1024]{2,1,0:T(8,128)(2,1)}, f32[2,1,512]{2,1,0:T(1,128)}) custom-call(bf16[2,512,512]{2,1,0:T(8,128)(2,1)} %points_ref.5, s32[2,1,128]{2,1,0:T(1,128)} %bitcast.102, bf16[512,1536]{1,0:T(8,128)(2,1)} %weight_ref.1), custom_call_target="tpu_custom_call" | custom-call | flops 1610612736 | bytes 4194304 | tf_op jit(solution)/shard_map/first_projection/pallas_call | solution.py:113
  8.3 0.5 collective-permute-start.3
  8.8 0.0 collective-permute-done.4
  8.8 0.0 collective-permute-done.5
  8.8 0.0 collective-permute-done.6
  8.8 1.3 collective-permute-start.7
  10.2 0.1 pad_add_fusion.2.here_ref
  10.2 1.1 collective-permute-done.7
  11.4 0.0 collective-permute-done.3.refs_1_
  11.4 0.0 copy-start.8
  11.4 0.1 collective-permute-start.8
  11.5 0.7 copy-done.8
  12.2 6.3 %first_attention.2 = (bf16[2,512,512]{2,1,0:T(8,128)(2,1)S(1)}, bf16[2,512,512]{2,1,0:T(8,128)(2,1)S(1)}) custom-call(bf16[2,512,512]{2,1,0:T(8,128)(2,1)} %get-tuple-element.98.query_ref, bf16[2,512,1024]{2,1,0:T(8,128)(2,1)} %get-tuple-element.99.kv_ref, f32[2,1,512]{2,1,0:T(1,128)} %get-tuple-element.100.bias_ref, bf16[2,512,512]{2,1,0:T(8,128)(2,1)} %points_ref.5, ...), custom_call_target="tpu_custom_call" | custom-call | flops 3221225472 | bytes 4194304 | tf_op jit(solution)/shard_map/first_attention/pallas_call | solution.py:181
  18.5 0.0 collective-permute-done.8
  18.6 2.4 %collective-permute-start.9 = (s32[2,8,256]{2,1,0:T(8,128)S(1)}, s32[2,8,256]{2,1,0:T(8,128)S(1)}, u32[]{:S(2)}, u32[]{:S(2)}) collective-permute-start(s32[2,8,256]{2,1,0:T(8,128)S(1)} %add_select_fusion.9), channel_id=1, source_target_pairs={{0,16},{2,18},{4,20},{6,22},{8,24},{10,26},{12,28},{14,30},{16,0},... | collective-permute-start | bytes 49160 | tf_op jit(solution)/shard_map/ppermute | solution.py:476
  21.0 6.3 %first_attention.3 = (bf16[2,512,512]{2,1,0:T(8,128)(2,1)S(1)}, bf16[2,512,512]{2,1,0:T(8,128)(2,1)S(1)}) custom-call(bf16[2,512,512]{2,1,0:T(8,128)(2,1)} %get-tuple-element.98.query_ref, bf16[2,512,1024]{2,1,0:T(8,128)(2,1)} %get-tuple-element.99.kv_ref, f32[2,1,512]{2,1,0:T(1,128)} %get-tuple-element.100.bias_ref, ...), custom_call_target="tpu_custom_call", output_to_operand_aliasing={{0}: (7, {}), {1}: (8, {})} | custom-call | flops 3221225472 | bytes 4194304 | tf_op jit(solution)/shard_map/first_attention/pallas_call | solution.py:181
  27.3 0.0 collective-permute-done.9
  27.4 1.7 %route.1 = (f32[32,128]{1,0:T(8,128)S(1)}, s32[8,256]{1,0:T(8,128)S(1)}, s32[1,1]{1,0:T(1,128)}) custom-call(s32[2]{0:T(128)S(1)} %pad_add_fusion.2.here_ref, s32[32,256]{1,0:T(8,128)S(1)} %bitcast.89), custom_call_target="tpu_custom_call" | custom-call | tf_op jit(solution)/shard_map/route/pallas_call | solution.py:626
  29.7 109.8 %conditional.1 = (bf16[2,512,512]{2,1,0:T(8,128)(2,1)}) conditional(s32[]{:T(128)} %bitcast.29, (s32[8,256]{1,0:T(8,128)S(1)}, bf16[1024,512]{1,0:T(8,128)(2,1)S(1)}, pred[]{:T(512)}, s32[2,16,256]{2,1,0:T(8,128)S(1)}, s32[2,16,256]{2,1,0:T(8,128)S(1)}, /*index=5*/s32[]{:T(128)}, bf16[512,1536]{1,0:T(8,128)(2,1)}, ...), branch_computations={%region_0.19_spmd, %region_19.20_spmd} | conditional | flops 27381792768 | bytes 65012156 | solution.py:847
  29.9 0.0 copy-start.12
  29.9 1.0 copy-done.12
  30.9 1.6 %pack.3 = bf16[512,512]{1,0:T(8,128)(2,1)} custom-call(s32[8,256]{1,0:T(8,128)S(1)} %get-tuple-element.55.slots_ref, bf16[1024,512]{1,0:T(8,128)(2,1)S(1)} %get-tuple-element.59.rows_ref), custom_call_target="tpu_custom_call" | custom-call | flops 536870912 | bytes 1048576 | tf_op jit(solution)/shard_map/cond/branch_1_fun/pack/pallas_call | solution.py:214
  32.5 1.5 %collective-permute-start = (bf16[512,512]{1,0:T(8,128)(2,1)}, bf16[512,512]{1,0:T(8,128)(2,1)S(1)}, u32[]{:S(2)}, u32[]{:S(2)}) collective-permute-start(bf16[512,512]{1,0:T(8,128)(2,1)} %pack.3), channel_id=1, source_target_pairs={{0,1},{1,0},{2,3},{3,2},{4,5},{5,4},{6,7},{7,6},{8,9},{9,8},{10,11... | collective-permute-start | bytes 1572872 | tf_op jit(solution)/shard_map/cond/branch_1_fun/ppermute | solution.py:749
  34.0 1.7 %collective-permute-done.taken_ref = bf16[512,512]{1,0:T(8,128)(2,1)S(1)} collective-permute-done((bf16[512,512]{1,0:T(8,128)(2,1)}, bf16[512,512]{1,0:T(8,128)(2,1)S(1)}, u32[]{:S(2)}, u32[]{:S(2)}) %collective-permute-start) | collective-permute-done | bytes 524320 | tf_op jit(solution)/shard_map/cond/branch_1_fun/ppermute | solution.py:749
  35.8 0.8 copy-done.2
  36.6 2.9 %pack_beside.1 = bf16[8,2,64,512]{3,2,1,0:T(8,128)(2,1)} custom-call(s32[2]{0:T(128)S(1)} %get-tuple-element.58.here_ref, s32[8,256]{1,0:T(8,128)S(1)} %get-tuple-element.55.slots_ref, bf16[1024,512]{1,0:T(8,128)(2,1)S(1)} %get-tuple-element.59.rows_ref, bf16[512,512]{1,0:T(8,128)(2,1)} %copy-done.2), custom_call_target="tpu_custom_call" | custom-call | flops 536870912 | bytes 2097152 | tf_op jit(solution)/shard_map/cond/branch_1_fun/pack_beside/pallas_call | solution.py:242
  39.5 4.6 %all-to-all-start = ((bf16[16,64,512]{2,1,0:T(8,128)(2,1)}), bf16[16,64,512]{2,1,0:T(8,128)(2,1)S(1)}, u32[]{:S(2)}, u32[]{:S(2)}) async-start(bf16[16,64,512]{2,1,0:T(8,128)(2,1)} %bitcast.75), calls=%async_computation | async-start | bytes 2097152 | tf_op jit(solution)/shard_map/cond/branch_1_fun/all_to_all | solution.py:493
  44.2 2.3 %plan.1 = (s32[1,256]{1,0:T(1,128)}, s32[8,128]{1,0:T(8,128)}, s32[8,128]{1,0:T(8,128)}, s32[1,1024]{1,0:T(1,128)}, s32[1,1024]{1,0:T(1,128)}) custom-call(s32[2]{0:T(128)S(1)} %get-tuple-element.58.here_ref, s32[32,256]{1,0:T(8,128)S(1)} %get-tuple-element.60.codes_ref, f32[32,128]{1,0:T(8,128)S(1)} %get-tuple-element.61.starts_ref), custom_call_target="tpu_custom_call" | custom-call | flops 8589934592 | bytes 4194304 | tf_op jit(solution)/shard_map/cond/branch_1_fun/plan/pallas_call | solution.py:731
  46.5 22.0 %all-to-all-done = bf16[16,64,512]{2,1,0:T(8,128)(2,1)S(1)} async-done(((bf16[16,64,512]{2,1,0:T(8,128)(2,1)}), bf16[16,64,512]{2,1,0:T(8,128)(2,1)S(1)}, u32[]{:S(2)}, u32[]{:S(2)}) %all-to-all-start) | async-done | bytes 1048608 | tf_op jit(solution)/shard_map/cond/branch_1_fun/all_to_all | solution.py:493
  68.4 2.4 %collective-permute-start.1 = (bf16[1024,512]{1,0:T(8,128)(2,1)S(1)}, bf16[1024,512]{1,0:T(8,128)(2,1)S(1)}, u32[]{:S(2)}, u32[]{:S(2)}) collective-permute-start(bf16[1024,512]{1,0:T(8,128)(2,1)S(1)} %bitcast.81), channel_id=1, source_target_pairs={{0,1},{1,0},{2,3},{3,2},{4,5},{5,4},{6,7},{7,6},{8,9},{9,8},{10,11... | collective-permute-start | bytes 3145736 | tf_op jit(solution)/shard_map/cond/branch_1_fun/ppermute | solution.py:749
  70.8 0.0 copy-done.1
  70.8 0.0 copy-done.4
  70.8 4.4 %arrange.3.query_ref = bf16[1024,512]{1,0:T(8,128)(2,1)} custom-call(s32[8,128]{1,0:T(8,128)} %get-tuple-element.67.limits_ref, bf16[1024,512]{1,0:T(8,128)(2,1)} %bitcast.82, s32[1,256]{1,0:T(1,128)} %get-tuple-element.69.place_ref, bf16[512,1536]{1,0:T(8,128)(2,1)S(1)} %copy-done.4), custom_call_target="tpu_custom_call" | custom-call | flops 1610612736 | bytes 2097152 | tf_op jit(solution)/shard_map/cond/branch_1_fun/arrange/pallas_call | solution.py:281
  75.2 0.0 collective-permute-done.1.refs_1_
  75.2 1.0 copy-done.5
  76.2 23.1 %rotated_attention.3 = bf16[1024,512]{1,0:T(8,128)(2,1)} custom-call(s32[8,128]{1,0:T(8,128)} %get-tuple-element.67.limits_ref, s32[8,128]{1,0:T(8,128)} %get-tuple-element.68.bounds_ref, s32[1,256]{1,0:T(1,128)} %get-tuple-element.69.place_ref, bf16[1024,512]{1,0:T(8,128)(2,1)} %arrange.3.query_ref, bf16[512,1536]{1,0:T(8,128)(2,1)S(1)} %copy-done.4, ...), custom_call_target="tpu_custom_call" | custom-call | flops 8589934592 | bytes 5242880 | tf_op jit(solution)/shard_map/cond/branch_1_fun/rotated_attention/pallas_call | solution.py:406
  99.4 5.7 %all-to-all-start.1 = ((bf16[16,64,512]{2,1,0:T(8,128)(2,1)}), bf16[16,64,512]{2,1,0:T(8,128)(2,1)S(1)}, u32[]{:S(2)}, u32[]{:S(2)}) async-start(bf16[16,64,512]{2,1,0:T(8,128)(2,1)} %bitcast.84), calls=%async_computation.1 | async-start | bytes 2097152 | tf_op jit(solution)/shard_map/cond/branch_1_fun/all_to_all | solution.py:493
  105.1 24.3 %all-to-all-done.1 = bf16[16,64,512]{2,1,0:T(8,128)(2,1)S(1)} async-done(((bf16[16,64,512]{2,1,0:T(8,128)(2,1)}), bf16[16,64,512]{2,1,0:T(8,128)(2,1)S(1)}, u32[]{:S(2)}, u32[]{:S(2)}) %all-to-all-start.1) | async-done | bytes 1048608 | tf_op jit(solution)/shard_map/cond/branch_1_fun/all_to_all | solution.py:493
  129.4 0.9 broadcast_select_fusion
  130.2 2.5 %collective-permute-start.2 = (bf16[512,512]{1,0:T(8,128)(2,1)S(1)}, bf16[512,512]{1,0:T(8,128)(2,1)S(1)}, u32[]{:S(2)}, u32[]{:S(2)}) collective-permute-start(bf16[512,512]{1,0:T(8,128)(2,1)S(1)} %bitcast.88), channel_id=1, source_target_pairs={{0,1},{1,0},{2,3},{3,2},{4,5},{5,4},{6,7},{7,6},{8,9},{9,8},{10,11... | collective-permute-start | bytes 1572872 | tf_op jit(solution)/shard_map/cond/branch_1_fun/ppermute | solution.py:749
  132.7 1.5 %collective-permute-done.2.refs_1_ = bf16[512,512]{1,0:T(8,128)(2,1)S(1)} collective-permute-done((bf16[512,512]{1,0:T(8,128)(2,1)S(1)}, bf16[512,512]{1,0:T(8,128)(2,1)S(1)}, u32[]{:S(2)}, u32[]{:S(2)}) %collective-permute-start.2) | collective-permute-done | bytes 524320 | tf_op jit(solution)/shard_map/cond/branch_1_fun/ppermute | solution.py:749
  134.2 0.8 copy-done.9
  135.1 0.0 copy-done.13
  135.1 4.5 %finish.3 = bf16[2,512,512]{2,1,0:T(8,128)(2,1)} custom-call(s32[8,256]{1,0:T(8,128)S(1)} %get-tuple-element.55.slots_ref, bf16[2,512,512]{2,1,0:T(8,128)(2,1)S(1)} %copy-done.13, bf16[512,512]{1,0:T(8,128)(2,1)S(1)} %copy-done.7, bf16[512,512]{1,0:T(8,128)(2,1)} %bitcast.87, bf16[512,512]{1,0:T(8,128)(2,1)} %copy-done.9), custom_call_target="tpu_custom_call" | custom-call | flops 1610612736 | bytes 4194304 | tf_op jit(solution)/shard_map/cond/branch_1_fun/finish/pallas_call | solution.py:451
  (17 shorter events, 0.1 us)
Async XLA Ops:
  0.7 8.1 %collective-permute-start.5 = (s32[1,1,256]{2,1,0:T(1,128)S(1)}, s32[1,1,256]{2,1,0:T(1,128)S(1)}, u32[]{:S(2)}, u32[]{:S(2)}) collective-permute-start(s32[1,1,256]{2,1,0:T(1,128)S(1)} %bitcast.97), channel_id=1, source_target_pairs={{0,2},{2,0},{4,6},{6,4},{8,10},{10,8},{12,14},{14,12},{16,18},{18,... | collective-permute-start | bytes 3080 | tf_op jit(solution)/shard_map/ppermute | solution.py:794
  1.9 6.9 %collective-permute-start.4 = (s32[1,1,256]{2,1,0:T(1,128)S(1)}, s32[1,1,256]{2,1,0:T(1,128)S(1)}, u32[]{:S(2)}, u32[]{:S(2)}) collective-permute-start(s32[1,1,256]{2,1,0:T(1,128)S(1)} %bitcast.98), channel_id=1, source_target_pairs={{0,1},{1,0},{2,3},{3,2},{4,5},{5,4},{6,7},{7,6},{8,9},{9,8},{10,11... | collective-permute-start | bytes 3080 | tf_op jit(solution)/shard_map/ppermute | solution.py:792
  2.9 5.9 %collective-permute-start.6 = (s32[1,1,256]{2,1,0:T(1,128)S(1)}, s32[1,1,256]{2,1,0:T(1,128)S(1)}, u32[]{:S(2)}, u32[]{:S(2)}) collective-permute-start(s32[1,1,256]{2,1,0:T(1,128)S(1)} %bitcast.99), channel_id=1, source_target_pairs={{0,3},{1,2},{2,1},{3,0},{4,7},{5,6},{6,5},{7,4},{8,11},{9,10},{10,... | collective-permute-start | bytes 3080 | tf_op jit(solution)/shard_map/ppermute | solution.py:794
  8.3 3.1 %collective-permute-start.3 = (bf16[2,128,1024]{2,1,0:T(8,128)(2,1)}, bf16[2,128,1024]{2,1,0:T(8,128)(2,1)S(1)}, u32[]{:S(2)}, u32[]{:S(2)}) collective-permute-start(bf16[2,128,1024]{2,1,0:T(8,128)(2,1)} %get-tuple-element.101.refs_0_), channel_id=1, source_target_pairs={{0,1},{1,0},{2,3},{3,2},{4,5},{5,4},{6,7},{7,6},{8,9},{9,8},{10,11... | collective-permute-start | bytes 1572872 | tf_op jit(solution)/shard_map/ppermute | solution.py:805
  8.8 2.5 %collective-permute-start.7 = (s32[2,2,256]{2,1,0:T(2,128)S(1)}, s32[2,2,256]{2,1,0:T(2,128)S(1)}, u32[]{:S(2)}, u32[]{:S(2)}) collective-permute-start(s32[2,2,256]{2,1,0:T(2,128)S(1)} %add_select_fusion.11), channel_id=1, source_target_pairs={{0,4},{2,6},{4,0},{6,2},{8,12},{10,14},{12,8},{14,10},{16,20},{18,... | collective-permute-start | bytes 12296 | tf_op jit(solution)/shard_map/ppermute | solution.py:476
  11.4 0.8 copy-start.8
  11.4 7.1 %collective-permute-start.8 = (s32[2,4,256]{2,1,0:T(4,128)S(1)}, s32[2,4,256]{2,1,0:T(4,128)S(1)}, u32[]{:S(2)}, u32[]{:S(2)}) collective-permute-start(s32[2,4,256]{2,1,0:T(4,128)S(1)} %add_select_fusion.10), channel_id=1, source_target_pairs={{0,8},{2,10},{4,12},{6,14},{8,0},{10,2},{12,4},{14,6},{16,24},{18,... | collective-permute-start | bytes 24584 | tf_op jit(solution)/shard_map/ppermute | solution.py:476
  18.6 8.7 %collective-permute-start.9 = (s32[2,8,256]{2,1,0:T(8,128)S(1)}, s32[2,8,256]{2,1,0:T(8,128)S(1)}, u32[]{:S(2)}, u32[]{:S(2)}) collective-permute-start(s32[2,8,256]{2,1,0:T(8,128)S(1)} %add_select_fusion.9), channel_id=1, source_target_pairs={{0,16},{2,18},{4,20},{6,22},{8,24},{10,26},{12,28},{14,30},{16,0},... | collective-permute-start | bytes 49160 | tf_op jit(solution)/shard_map/ppermute | solution.py:476
  29.9 1.0 copy-start.12
  32.5 3.2 %collective-permute-start = (bf16[512,512]{1,0:T(8,128)(2,1)}, bf16[512,512]{1,0:T(8,128)(2,1)S(1)}, u32[]{:S(2)}, u32[]{:S(2)}) collective-permute-start(bf16[512,512]{1,0:T(8,128)(2,1)} %pack.3), channel_id=1, source_target_pairs={{0,1},{1,0},{2,3},{3,2},{4,5},{5,4},{6,7},{7,6},{8,9},{9,8},{10,11... | collective-permute-start | bytes 1572872 | tf_op jit(solution)/shard_map/cond/branch_1_fun/ppermute | solution.py:749
  35.8 0.8 copy-start.2
  39.5 28.9 %all-to-all-start = ((bf16[16,64,512]{2,1,0:T(8,128)(2,1)}), bf16[16,64,512]{2,1,0:T(8,128)(2,1)S(1)}, u32[]{:S(2)}, u32[]{:S(2)}) async-start(bf16[16,64,512]{2,1,0:T(8,128)(2,1)} %bitcast.75), calls=%async_computation | async-start | bytes 2097152 | tf_op jit(solution)/shard_map/cond/branch_1_fun/all_to_all | solution.py:493
  44.2 26.7 %copy-start.4 = (bf16[512,1536]{1,0:T(8,128)(2,1)S(1)}, bf16[512,1536]{1,0:T(8,128)(2,1)}, u32[]{:S(2)}) copy-start(bf16[512,1536]{1,0:T(8,128)(2,1)} %get-tuple-element.71.weight_ref.key_weight_ref.value_weight_ref) | copy-start | bytes 4718596 | tf_op jit(solution)/shard_map/cond
  68.4 2.4 %copy-start.1 = (bf16[16,64,512]{2,1,0:T(8,128)(2,1)}, bf16[16,64,512]{2,1,0:T(8,128)(2,1)S(1)}, u32[]{:S(2)}) copy-start(bf16[16,64,512]{2,1,0:T(8,128)(2,1)S(1)} %all-to-all-done) | copy-start | bytes 3145732 | tf_op jit(solution)/shard_map/cond
  68.4 6.8 %collective-permute-start.1 = (bf16[1024,512]{1,0:T(8,128)(2,1)S(1)}, bf16[1024,512]{1,0:T(8,128)(2,1)S(1)}, u32[]{:S(2)}, u32[]{:S(2)}) collective-permute-start(bf16[1024,512]{1,0:T(8,128)(2,1)S(1)} %bitcast.81), channel_id=1, source_target_pairs={{0,1},{1,0},{2,3},{3,2},{4,5},{5,4},{6,7},{7,6},{8,9},{9,8},{10,11... | collective-permute-start | bytes 3145736 | tf_op jit(solution)/shard_map/cond/branch_1_fun/ppermute | solution.py:749
  75.2 1.0 copy-start.5
  99.4 35.7 %copy-start.7 = (bf16[512,512]{1,0:T(8,128)(2,1)S(1)}, bf16[512,512]{1,0:T(8,128)(2,1)}, u32[]{:S(2)}) copy-start(bf16[512,512]{1,0:T(8,128)(2,1)} %get-tuple-element.57.weight_ref) | copy-start | bytes 1572868 | tf_op jit(solution)/shard_map/cond
  99.4 35.7 %copy-start.13 = (bf16[2,512,512]{2,1,0:T(8,128)(2,1)S(1)}, bf16[2,512,512]{2,1,0:T(8,128)(2,1)}, u32[]{:S(2)}) copy-start(bf16[2,512,512]{2,1,0:T(8,128)(2,1)} %copy-done.12) | copy-start | bytes 3145732 | tf_op jit(solution)/shard_map/cond
  99.4 30.0 %all-to-all-start.1 = ((bf16[16,64,512]{2,1,0:T(8,128)(2,1)}), bf16[16,64,512]{2,1,0:T(8,128)(2,1)S(1)}, u32[]{:S(2)}, u32[]{:S(2)}) async-start(bf16[16,64,512]{2,1,0:T(8,128)(2,1)} %bitcast.84), calls=%async_computation.1 | async-start | bytes 2097152 | tf_op jit(solution)/shard_map/cond/branch_1_fun/all_to_all | solution.py:493
  130.2 4.0 %collective-permute-start.2 = (bf16[512,512]{1,0:T(8,128)(2,1)S(1)}, bf16[512,512]{1,0:T(8,128)(2,1)S(1)}, u32[]{:S(2)}, u32[]{:S(2)}) collective-permute-start(bf16[512,512]{1,0:T(8,128)(2,1)S(1)} %bitcast.88), channel_id=1, source_target_pairs={{0,1},{1,0},{2,3},{3,2},{4,5},{5,4},{6,7},{7,6},{8,9},{9,8},{10,11... | collective-permute-start | bytes 1572872 | tf_op jit(solution)/shard_map/cond/branch_1_fun/ppermute | solution.py:749
  134.2 0.8 copy-start.9
where the time goes:
time: 141 us; the launch traced here: 140 us
  Pallas kernels  58.5 us (41%)
  waiting for transfers between devices  50.7 us (36%)
  starting transfers between devices  23.3 us (17%)
  local copies, waits for them, and re-layouts  4.33 us (3%)
  other arithmetic  1.71 us (1%)
    all_to_all x2, waiting for transfers between devices, exchange(): lax.all_to_all(parts, 'wide', split_axis=0, concat_axis=0, tiled=True)  46.3 us
    pallas_call x1, Pallas kernels, rotated_attention(): pl.pallas_call(functools.partial(rotated_attention_kernel, len(parts), st...  23.1 us
    pallas_call x2, Pallas kernels, first_attention(): pl.pallas_call(functools.partial(first_attention_kernel, width, len(coars...  12.7 us
    all_to_all x2, starting transfers between devices, exchange(): lax.all_to_all(parts, 'wide', split_axis=0, concat_axis=0, tiled=True)  10.4 us
    ppermute x3, starting transfers between devices, by_chips(): swap = lambda array: lax.ppermute(array, 'narrow', [(0, 1), (1, 0)])  6.34 us
    pallas_call x1, Pallas kernels, first_projection(): pl.pallas_call(functools.partial(first_projection_kernel, width), grid=(b...  5.25 us
    pallas_call x1, Pallas kernels, finish(): pl.pallas_call(functools.partial(finish_kernel, route_index), grid=(balls...  4.46 us
    pallas_call x1, Pallas kernels, arrange(): pl.pallas_call(functools.partial(arrange_kernel, factor), grid=(count //...  4.38 us
  transfers between devices with their start and end apart: 12, of which 5 were waited for; matrix products, arithmetic and copies ran while one was open for 0% of the time, Pallas kernels for 18%

commit v1 on v0

--- a/solution.py
+++ b/solution.py
@@ -425,7 +425,7 @@
     )(limits, bounds, place, query, weight, weight, *parts, *key_places)
 
 
-def finish_kernel(route_index, slots_ref, layer_ref, weight_ref, *refs):
+def finish_kernel(route_index, here_ref, slots_ref, layer_ref, weight_ref, *refs):
     returned, result_ref, all_slots = refs[:-2], refs[-2], refs[-1]
     share = layer_ref.shape[1]
 
@@ -436,33 +436,42 @@
     slot = all_slots[pl.ds(pl.multiple_of(pl.program_id(0) * share, share), share), :]
     attended, first = None, 0
     for part in returned:
-        target = first + iota((share, part.shape[0]), 1)
-        found = mm(jnp.where(target == slot, 1.0, 0.0).astype(BF16), part[...])
+        rows = part[...].reshape(-1, part.shape[-1])
+        target = first + iota((share, rows.shape[0]), 1)
+        found = mm(jnp.where(target == slot, 1.0, 0.0).astype(BF16), rows)
         attended = found if attended is None else attended + found
-        first += part.shape[0]
+        first += rows.shape[0]
     layer = layer_ref[0].astype(F32)
     result_ref[0] = (layer + mm(attended.astype(BF16), weight_ref[...])).astype(BF16)
 
 
-def finish(slots, route_index, layer, weight, returned):
+def finish(here, slots, route_index, layer, weight, returned):
     balls, share, width = layer.shape
-    ball = lambda rows, cols: pl.BlockSpec((1, rows, cols), lambda b: (b, 0, 0))
-    rows = sum(part.shape[0] for part in returned)
+    full = lambda shape: pl.BlockSpec(shape, lambda b, here: (0,) * len(shape))
+    ball = pl.BlockSpec((1, share, width), lambda b, here: (b, 0, 0))
+
+    def of_core(shape):
+        return pl.BlockSpec((shape[0], 1) + shape[2:], lambda b, here: (0, here[0], 0, 0))
+
+    rows = sum(part.size // width // (2 if part.ndim == 4 else 1) for part in returned)
     return pl.pallas_call(
         functools.partial(finish_kernel, route_index),
-        grid=(balls,),
-        in_specs=[whole(slots), ball(share, width), whole(weight)]
-        + [whole(part) for part in returned],
-        out_specs=ball(share, width),
+        grid_spec=pltpu.PrefetchScalarGridSpec(
+            num_scalar_prefetch=1,
+            grid=(balls,),
+            in_specs=[full(slots.shape), ball, full(weight.shape)]
+            + [of_core(part.shape) if part.ndim == 4 else full(part.shape) for part in returned],
+            out_specs=ball,
+            scratch_shapes=[pltpu.VMEM((balls * share, 1), I32)],
+        ),
         out_shape=jax.ShapeDtypeStruct(layer.shape, BF16),
-        scratch_shapes=[pltpu.VMEM((balls * share, 1), I32)],
         compiler_params=params(),
         cost_estimate=pl.CostEstimate(
             flops=2 * balls * share * width * (rows + width),
             bytes_accessed=8 * balls * share * width, transcendentals=0,
         ),
         name="finish",
-    )(slots, layer, weight, *returned)
+    )(here, slots, layer, weight, *returned)
 
 
 def side_by_side(mine, other, lower, axis):
@@ -749,11 +758,6 @@
     swap = lambda array: lax.ppermute(array, "narrow", [(0, 1), (1, 0)])
     is_first = lax.axis_index("narrow") == 0
 
-    def take_apart(array):
-        both = array.reshape(units, 2, rows_half // units, -1)
-        low, high = both[:, 0].reshape(rows_half, -1), both[:, 1].reshape(rows_half, -1)
-        return jnp.where(is_first, low, high), jnp.where(is_first, high, low)
-
     taken = swap(pack(slots, 0, normed, rows_half, rows_half))
     arrived = exchange(pack_beside(here, slots, normed, taken, units), wide_count)
     tile = min(TILE, 2 * rows_half)
@@ -764,8 +768,9 @@
     key_rows = 4 * rows_half
 
     mixture = rotated_attention(places, query, [arrived, partner], weight, key_rows, 6)
-    kept, given = take_apart(exchange(mixture, wide_count))
-    return [kept, swap(given)]
+    both = exchange(mixture, wide_count).reshape(units, 2, rows_half // units, -1)
+    given = jnp.where(is_first, both[:, 1], both[:, 0]).reshape(rows_half, -1)
+    return [both, swap(given)]
 
 
 def on_device(
@@ -822,24 +827,25 @@
     layer_one, normed = results
     normed = normed.reshape(balls * share, width)
 
+    core = lax.axis_index("narrow")
+    here = jnp.stack([core, lax.axis_index("wide")]).astype(I32)
+
     def slot_route(codes, slots, route_index):
         index = lax.axis_index("wide")
         returned = by_slots(normed, slots, route_index, codes, index, capacity, qkv_second)
-        return finish(slots, route_index, layer_one, out_second, returned)
+        return finish(here, slots, route_index, layer_one, out_second, returned)
 
     if not paired:
         onehot = (jnp.arange(wide_count, dtype=I32)[:, None] == dest_flat[None, :]).astype(I32)
         rank = jnp.sum(earlier_sum(onehot) * onehot, axis=0, dtype=I32)
         return slot_route(codes[0], (dest_flat * capacity + rank).reshape(1, -1), 0)
 
-    core = lax.axis_index("narrow")
-    here = jnp.stack([core, lax.axis_index("wide")]).astype(I32)
     unit = 2 * block_count // wide_count
     codes = codes.reshape(2 * wide_count, block_count)
     starts, slots, straddle = route(codes, here, wide_count, capacity, unit)
     def chip_route():
         returned = by_chips(normed, slots, here, codes, starts, qkv_second)
-        return finish(slots, 0, layer_one, out_second, returned)
+        return finish(here, slots, 0, layer_one, out_second, returned)
 
     def own_labels():
         return codes.reshape(2, wide_count, block_count)[core]

time: 141 us -> 140 us (level)
  no operation moved by 1% of the time
where the time goes in v1:
time: 140 us; the launch traced here: 137 us
  Pallas kernels  59.2 us (42%)
  waiting for transfers between devices  50.7 us (36%)
  starting transfers between devices  22.1 us (16%)
  local copies, waits for them, and re-layouts  3.38 us (2%)
    all_to_all x2, waiting for transfers between devices, exchange(): lax.all_to_all(parts, 'wide', split_axis=0, concat_axis=0, tiled=True)  46.3 us
    pallas_call x1, Pallas kernels, rotated_attention(): pl.pallas_call(functools.partial(rotated_attention_kernel, len(parts), st...  23.2 us
    pallas_call x2, Pallas kernels, first_attention(): pl.pallas_call(functools.partial(first_attention_kernel, width, len(coars...  12.7 us
    all_to_all x2, starting transfers between devices, exchange(): lax.all_to_all(parts, 'wide', split_axis=0, concat_axis=0, tiled=True)  9.17 us
    ppermute x3, starting transfers between devices, by_chips(): swap = lambda array: lax.ppermute(array, 'narrow', [(0, 1), (1, 0)])  6.41 us
    pallas_call x1, Pallas kernels, first_projection(): pl.pallas_call(functools.partial(first_projection_kernel, width), grid=(b...  5.25 us
    pallas_call x1, Pallas kernels, finish(): pl.pallas_call(functools.partial(finish_kernel, route_index), grid_spec=p...  5.04 us
    pallas_call x1, Pallas kernels, arrange(): pl.pallas_call(functools.partial(arrange_kernel, factor), grid=(count //...  4.37 us
  transfers between devices with their start and end apart: 12, of which 5 were waited for; matrix products, arithmetic and copies ran while one was open for 0% of the time, Pallas kernels for 18%

profile of v1, /device:TPU:9, one launch (start us, length us, event | category | flops | bytes accessed | tf_op | source)
XLA Modules:
  0.0 137.3 jit_solution(13986956186317230372)
XLA Ops:
  0.0 0.7 add_add_fusion.1
  0.7 1.2 collective-permute-start.5
  1.9 1.0 collective-permute-start.4
  2.9 0.1 collective-permute-start.6
  3.0 5.2 %first_projection.1 = (bf16[2,512,512]{2,1,0:T(8,128)(2,1)}, bf16[2,512,1024]{2,1,0:T(8,128)(2,1)}, bf16[2,128,1024]{2,1,0:T(8,128)(2,1)}, f32[2,1,512]{2,1,0:T(1,128)}) custom-call(bf16[2,512,512]{2,1,0:T(8,128)(2,1)} %points_ref.5, s32[2,1,128]{2,1,0:T(1,128)} %bitcast.101, bf16[512,1536]{1,0:T(8,128)(2,1)} %weight_ref.1), custom_call_target="tpu_custom_call" | custom-call | flops 1610612736 | bytes 4194304 | tf_op jit(solution)/shard_map/first_projection/pallas_call | solution.py:113
  8.3 0.5 collective-permute-start.3
  8.8 0.0 collective-permute-done.4
  8.8 0.0 collective-permute-done.5
  8.8 0.0 collective-permute-done.6
  8.8 1.3 collective-permute-start.7
  10.2 0.1 pad_add_fusion.2.here_ref
  10.2 1.1 collective-permute-done.7
  11.4 0.0 collective-permute-done.3.refs_1_
  11.4 0.0 copy-start.8
  11.4 0.1 collective-permute-start.8
  11.5 0.7 copy-done.8
  12.2 6.3 %first_attention.2 = (bf16[2,512,512]{2,1,0:T(8,128)(2,1)S(1)}, bf16[2,512,512]{2,1,0:T(8,128)(2,1)S(1)}) custom-call(bf16[2,512,512]{2,1,0:T(8,128)(2,1)} %get-tuple-element.101.query_ref, bf16[2,512,1024]{2,1,0:T(8,128)(2,1)} %get-tuple-element.102.kv_ref, f32[2,1,512]{2,1,0:T(1,128)} %get-tuple-element.103.bias_ref, bf16[2,512,512]{2,1,0:T(8,128)(2,1)} %points_ref.5, ...), custom_call_target="tpu_custom_call" | custom-call | flops 3221225472 | bytes 4194304 | tf_op jit(solution)/shard_map/first_attention/pallas_call | solution.py:181
  18.5 0.0 collective-permute-done.8
  18.6 2.4 %collective-permute-start.9 = (s32[2,8,256]{2,1,0:T(8,128)S(1)}, s32[2,8,256]{2,1,0:T(8,128)S(1)}, u32[]{:S(2)}, u32[]{:S(2)}) collective-permute-start(s32[2,8,256]{2,1,0:T(8,128)S(1)} %add_select_fusion.9), channel_id=1, source_target_pairs={{0,16},{2,18},{4,20},{6,22},{8,24},{10,26},{12,28},{14,30},{16,0},... | collective-permute-start | bytes 49160 | tf_op jit(solution)/shard_map/ppermute | solution.py:485
  21.0 6.4 %first_attention.3 = (bf16[2,512,512]{2,1,0:T(8,128)(2,1)S(1)}, bf16[2,512,512]{2,1,0:T(8,128)(2,1)S(1)}) custom-call(bf16[2,512,512]{2,1,0:T(8,128)(2,1)} %get-tuple-element.101.query_ref, bf16[2,512,1024]{2,1,0:T(8,128)(2,1)} %get-tuple-element.102.kv_ref, f32[2,1,512]{2,1,0:T(1,128)} %get-tuple-element.103.bias_ref, ...), custom_call_target="tpu_custom_call", output_to_operand_aliasing={{0}: (7, {}), {1}: (8, {})} | custom-call | flops 3221225472 | bytes 4194304 | tf_op jit(solution)/shard_map/first_attention/pallas_call | solution.py:181
  27.4 0.0 collective-permute-done.9
  27.4 1.7 %route.1 = (f32[32,128]{1,0:T(8,128)S(1)}, s32[8,256]{1,0:T(8,128)S(1)}, s32[1,1]{1,0:T(1,128)}) custom-call(s32[2]{0:T(128)S(1)} %pad_add_fusion.2.here_ref, s32[32,256]{1,0:T(8,128)S(1)} %bitcast.88), custom_call_target="tpu_custom_call" | custom-call | tf_op jit(solution)/shard_map/route/pallas_call | solution.py:635
  29.8 0.0 copy-done.7
  29.8 107.6 %conditional.1 = (bf16[2,512,512]{2,1,0:T(8,128)(2,1)}) conditional(s32[]{:T(128)} %bitcast.28, (s32[8,256]{1,0:T(8,128)S(1)}, bf16[1024,512]{1,0:T(8,128)(2,1)S(1)}, pred[]{:T(512)}, s32[2,16,256]{2,1,0:T(8,128)S(1)}, s32[2,16,256]{2,1,0:T(8,128)S(1)}, /*index=5*/s32[]{:T(128)}, bf16[512,1536]{1,0:T(8,128)(2,1)}, s32[2]{0:T(128)S(1)}, ...), branch_computations={%region_0.19_spmd, %region_19.20_spmd} | conditional | flops 27381792768 | bytes 66585020 | solution.py:853
  30.0 0.0 copy-start.12
  30.0 1.6 %pack.3 = bf16[512,512]{1,0:T(8,128)(2,1)} custom-call(s32[8,256]{1,0:T(8,128)S(1)} %get-tuple-element.59.slots_ref, bf16[1024,512]{1,0:T(8,128)(2,1)S(1)} %get-tuple-element.62.rows_ref), custom_call_target="tpu_custom_call" | custom-call | flops 536870912 | bytes 1048576 | tf_op jit(solution)/shard_map/cond/branch_1_fun/pack/pallas_call | solution.py:214
  31.7 1.5 %collective-permute-start = (bf16[512,512]{1,0:T(8,128)(2,1)}, bf16[512,512]{1,0:T(8,128)(2,1)S(1)}, u32[]{:S(2)}, u32[]{:S(2)}) collective-permute-start(bf16[512,512]{1,0:T(8,128)(2,1)} %pack.3), channel_id=1, source_target_pairs={{0,1},{1,0},{2,3},{3,2},{4,5},{5,4},{6,7},{7,6},{8,9},{9,8},{10,11... | collective-permute-start | bytes 1572872 | tf_op jit(solution)/shard_map/cond/branch_1_fun/ppermute | solution.py:758
  33.1 1.7 %collective-permute-done.taken_ref = bf16[512,512]{1,0:T(8,128)(2,1)S(1)} collective-permute-done((bf16[512,512]{1,0:T(8,128)(2,1)}, bf16[512,512]{1,0:T(8,128)(2,1)S(1)}, u32[]{:S(2)}, u32[]{:S(2)}) %collective-permute-start) | collective-permute-done | bytes 524320 | tf_op jit(solution)/shard_map/cond/branch_1_fun/ppermute | solution.py:758
  34.9 0.8 copy-done.3
  35.7 2.9 %pack_beside.1 = bf16[8,2,64,512]{3,2,1,0:T(8,128)(2,1)} custom-call(s32[2]{0:T(128)S(1)} %get-tuple-element.58.here_ref, s32[8,256]{1,0:T(8,128)S(1)} %get-tuple-element.59.slots_ref, bf16[1024,512]{1,0:T(8,128)(2,1)S(1)} %get-tuple-element.62.rows_ref, bf16[512,512]{1,0:T(8,128)(2,1)} %copy-done.3), custom_call_target="tpu_custom_call" | custom-call | flops 536870912 | bytes 2097152 | tf_op jit(solution)/shard_map/cond/branch_1_fun/pack_beside/pallas_call | solution.py:242
  38.6 0.0 copy-done.12
  38.6 4.6 %all-to-all-start = ((bf16[16,64,512]{2,1,0:T(8,128)(2,1)}), bf16[16,64,512]{2,1,0:T(8,128)(2,1)S(1)}, u32[]{:S(2)}, u32[]{:S(2)}) async-start(bf16[16,64,512]{2,1,0:T(8,128)(2,1)} %bitcast.75), calls=%async_computation | async-start | bytes 2097152 | tf_op jit(solution)/shard_map/cond/branch_1_fun/all_to_all | solution.py:502
  43.3 2.3 %plan.1 = (s32[1,256]{1,0:T(1,128)}, s32[8,128]{1,0:T(8,128)}, s32[8,128]{1,0:T(8,128)}, s32[1,1024]{1,0:T(1,128)}, s32[1,1024]{1,0:T(1,128)}) custom-call(s32[2]{0:T(128)S(1)} %get-tuple-element.58.here_ref, s32[32,256]{1,0:T(8,128)S(1)} %get-tuple-element.63.codes_ref, f32[32,128]{1,0:T(8,128)S(1)} %get-tuple-element.64.starts_ref), custom_call_target="tpu_custom_call" | custom-call | flops 8589934592 | bytes 4194304 | tf_op jit(solution)/shard_map/cond/branch_1_fun/plan/pallas_call | solution.py:740
  45.6 22.0 %all-to-all-done = bf16[16,64,512]{2,1,0:T(8,128)(2,1)S(1)} async-done(((bf16[16,64,512]{2,1,0:T(8,128)(2,1)}), bf16[16,64,512]{2,1,0:T(8,128)(2,1)S(1)}, u32[]{:S(2)}, u32[]{:S(2)}) %all-to-all-start) | async-done | bytes 1048608 | tf_op jit(solution)/shard_map/cond/branch_1_fun/all_to_all | solution.py:502
  67.6 2.4 %collective-permute-start.1 = (bf16[1024,512]{1,0:T(8,128)(2,1)S(1)}, bf16[1024,512]{1,0:T(8,128)(2,1)S(1)}, u32[]{:S(2)}, u32[]{:S(2)}) collective-permute-start(bf16[1024,512]{1,0:T(8,128)(2,1)S(1)} %bitcast.81), channel_id=1, source_target_pairs={{0,1},{1,0},{2,3},{3,2},{4,5},{5,4},{6,7},{7,6},{8,9},{9,8},{10,11... | collective-permute-start | bytes 3145736 | tf_op jit(solution)/shard_map/cond/branch_1_fun/ppermute | solution.py:758
  70.0 0.0 copy-done.2
  70.0 0.0 copy-done.5
  70.0 4.4 %arrange.3.query_ref = bf16[1024,512]{1,0:T(8,128)(2,1)} custom-call(s32[8,128]{1,0:T(8,128)} %get-tuple-element.70.limits_ref, bf16[1024,512]{1,0:T(8,128)(2,1)} %bitcast.82, s32[1,256]{1,0:T(1,128)} %get-tuple-element.72.place_ref, bf16[512,1536]{1,0:T(8,128)(2,1)S(1)} %copy-done.5), custom_call_target="tpu_custom_call" | custom-call | flops 1610612736 | bytes 2097152 | tf_op jit(solution)/shard_map/cond/branch_1_fun/arrange/pallas_call | solution.py:281
  74.3 0.0 collective-permute-done.1.refs_1_
  74.3 1.0 copy-done.6
  75.3 23.2 %rotated_attention.3 = bf16[1024,512]{1,0:T(8,128)(2,1)} custom-call(s32[8,128]{1,0:T(8,128)} %get-tuple-element.70.limits_ref, s32[8,128]{1,0:T(8,128)} %get-tuple-element.71.bounds_ref, s32[1,256]{1,0:T(1,128)} %get-tuple-element.72.place_ref, bf16[1024,512]{1,0:T(8,128)(2,1)} %arrange.3.query_ref, bf16[512,1536]{1,0:T(8,128)(2,1)S(1)} %copy-done.5, ...), custom_call_target="tpu_custom_call" | custom-call | flops 8589934592 | bytes 5242880 | tf_op jit(solution)/shard_map/cond/branch_1_fun/rotated_attention/pallas_call | solution.py:406
  98.5 4.5 %all-to-all-start.1 = ((bf16[16,64,512]{2,1,0:T(8,128)(2,1)}), bf16[16,64,512]{2,1,0:T(8,128)(2,1)S(1)}, u32[]{:S(2)}, u32[]{:S(2)}) async-start(bf16[16,64,512]{2,1,0:T(8,128)(2,1)} %bitcast.84), calls=%async_computation.1 | async-start | bytes 2097152 | tf_op jit(solution)/shard_map/cond/branch_1_fun/all_to_all | solution.py:502
  103.1 24.3 %all-to-all-done.1 = bf16[16,64,512]{2,1,0:T(8,128)(2,1)S(1)} async-done(((bf16[16,64,512]{2,1,0:T(8,128)(2,1)}), bf16[16,64,512]{2,1,0:T(8,128)(2,1)S(1)}, u32[]{:S(2)}, u32[]{:S(2)}) %all-to-all-start.1) | async-done | bytes 1048608 | tf_op jit(solution)/shard_map/cond/branch_1_fun/all_to_all | solution.py:502
  127.4 0.1 slice_select_fusion
  127.4 2.5 %collective-permute-start.2 = (bf16[512,512]{1,0:T(8,128)(2,1)S(1)}, bf16[512,512]{1,0:T(8,128)(2,1)S(1)}, u32[]{:S(2)}, u32[]{:S(2)}) collective-permute-start(bf16[512,512]{1,0:T(8,128)(2,1)S(1)} %bitcast.87), channel_id=1, source_target_pairs={{0,1},{1,0},{2,3},{3,2},{4,5},{5,4},{6,7},{7,6},{8,9},{9,8},{10,11... | collective-permute-start | bytes 1572872 | tf_op jit(solution)/shard_map/cond/branch_1_fun/ppermute | solution.py:758
  129.9 1.5 %collective-permute-done.2.refs_1_ = bf16[512,512]{1,0:T(8,128)(2,1)S(1)} collective-permute-done((bf16[512,512]{1,0:T(8,128)(2,1)S(1)}, bf16[512,512]{1,0:T(8,128)(2,1)S(1)}, u32[]{:S(2)}, u32[]{:S(2)}) %collective-permute-start.2) | collective-permute-done | bytes 524320 | tf_op jit(solution)/shard_map/cond/branch_1_fun/ppermute | solution.py:758
  131.5 0.8 copy-done.9
  132.3 5.0 %finish.3 = bf16[2,512,512]{2,1,0:T(8,128)(2,1)} custom-call(s32[2]{0:T(128)S(1)} %get-tuple-element.58.here_ref, s32[8,256]{1,0:T(8,128)S(1)} %get-tuple-element.59.slots_ref, bf16[2,512,512]{2,1,0:T(8,128)(2,1)S(1)} %copy-done.13, bf16[512,512]{1,0:T(8,128)(2,1)S(1)} %get-tuple-element.61.weight_ref, bf16[8,2,64,512]{3,2,1,0:T(8,128)(2,1)} %bitcast.74, ...), custom_call_target="tpu_custom_call" | custom-call | flops 1610612736 | bytes 4194304 | tf_op jit(solution)/shard_map/cond/branch_1_fun/finish/pallas_call | solution.py:457
  (19 shorter events, 0.1 us)
Async XLA Ops:
  0.7 8.1 %collective-permute-start.5 = (s32[1,1,256]{2,1,0:T(1,128)S(1)}, s32[1,1,256]{2,1,0:T(1,128)S(1)}, u32[]{:S(2)}, u32[]{:S(2)}) collective-permute-start(s32[1,1,256]{2,1,0:T(1,128)S(1)} %bitcast.96), channel_id=1, source_target_pairs={{0,2},{2,0},{4,6},{6,4},{8,10},{10,8},{12,14},{14,12},{16,18},{18,... | collective-permute-start | bytes 3080 | tf_op jit(solution)/shard_map/ppermute | solution.py:799
  1.9 6.9 %collective-permute-start.4 = (s32[1,1,256]{2,1,0:T(1,128)S(1)}, s32[1,1,256]{2,1,0:T(1,128)S(1)}, u32[]{:S(2)}, u32[]{:S(2)}) collective-permute-start(s32[1,1,256]{2,1,0:T(1,128)S(1)} %bitcast.97), channel_id=1, source_target_pairs={{0,1},{1,0},{2,3},{3,2},{4,5},{5,4},{6,7},{7,6},{8,9},{9,8},{10,11... | collective-permute-start | bytes 3080 | tf_op jit(solution)/shard_map/ppermute | solution.py:797
  2.9 5.9 %collective-permute-start.6 = (s32[1,1,256]{2,1,0:T(1,128)S(1)}, s32[1,1,256]{2,1,0:T(1,128)S(1)}, u32[]{:S(2)}, u32[]{:S(2)}) collective-permute-start(s32[1,1,256]{2,1,0:T(1,128)S(1)} %bitcast.98), channel_id=1, source_target_pairs={{0,3},{1,2},{2,1},{3,0},{4,7},{5,6},{6,5},{7,4},{8,11},{9,10},{10,... | collective-permute-start | bytes 3080 | tf_op jit(solution)/shard_map/ppermute | solution.py:799
  8.3 3.1 %collective-permute-start.3 = (bf16[2,128,1024]{2,1,0:T(8,128)(2,1)}, bf16[2,128,1024]{2,1,0:T(8,128)(2,1)S(1)}, u32[]{:S(2)}, u32[]{:S(2)}) collective-permute-start(bf16[2,128,1024]{2,1,0:T(8,128)(2,1)} %get-tuple-element.104.refs_0_), channel_id=1, source_target_pairs={{0,1},{1,0},{2,3},{3,2},{4,5},{5,4},{6,7},{7,6},{8,9},{9,8},{10,11... | collective-permute-start | bytes 1572872 | tf_op jit(solution)/shard_map/ppermute | solution.py:810
  8.8 2.5 %collective-permute-start.7 = (s32[2,2,256]{2,1,0:T(2,128)S(1)}, s32[2,2,256]{2,1,0:T(2,128)S(1)}, u32[]{:S(2)}, u32[]{:S(2)}) collective-permute-start(s32[2,2,256]{2,1,0:T(2,128)S(1)} %add_select_fusion.11), channel_id=1, source_target_pairs={{0,4},{2,6},{4,0},{6,2},{8,12},{10,14},{12,8},{14,10},{16,20},{18,... | collective-permute-start | bytes 12296 | tf_op jit(solution)/shard_map/ppermute | solution.py:485
  11.4 0.8 copy-start.8
  11.4 7.1 %collective-permute-start.8 = (s32[2,4,256]{2,1,0:T(4,128)S(1)}, s32[2,4,256]{2,1,0:T(4,128)S(1)}, u32[]{:S(2)}, u32[]{:S(2)}) collective-permute-start(s32[2,4,256]{2,1,0:T(4,128)S(1)} %add_select_fusion.10), channel_id=1, source_target_pairs={{0,8},{2,10},{4,12},{6,14},{8,0},{10,2},{12,4},{14,6},{16,24},{18,... | collective-permute-start | bytes 24584 | tf_op jit(solution)/shard_map/ppermute | solution.py:485
  18.6 8.8 %collective-permute-start.9 = (s32[2,8,256]{2,1,0:T(8,128)S(1)}, s32[2,8,256]{2,1,0:T(8,128)S(1)}, u32[]{:S(2)}, u32[]{:S(2)}) collective-permute-start(s32[2,8,256]{2,1,0:T(8,128)S(1)} %add_select_fusion.9), channel_id=1, source_target_pairs={{0,16},{2,18},{4,20},{6,22},{8,24},{10,26},{12,28},{14,30},{16,0},... | collective-permute-start | bytes 49160 | tf_op jit(solution)/shard_map/ppermute | solution.py:485
  21.0 8.8 %copy-start.7 = (bf16[512,512]{1,0:T(8,128)(2,1)S(1)}, bf16[512,512]{1,0:T(8,128)(2,1)}, u32[]{:S(2)}) copy-start(bf16[512,512]{1,0:T(8,128)(2,1)} %param.17) | copy-start | bytes 1572868
  30.0 8.6 %copy-start.12 = (bf16[2,512,512]{2,1,0:T(8,128)(2,1)}, bf16[2,512,512]{2,1,0:T(8,128)(2,1)S(1)}, u32[]{:S(2)}) copy-start(bf16[2,512,512]{2,1,0:T(8,128)(2,1)S(1)} %get-tuple-element.60.layer_ref) | copy-start | bytes 3145732 | tf_op jit(solution)/shard_map/cond
  31.7 3.2 %collective-permute-start = (bf16[512,512]{1,0:T(8,128)(2,1)}, bf16[512,512]{1,0:T(8,128)(2,1)S(1)}, u32[]{:S(2)}, u32[]{:S(2)}) collective-permute-start(bf16[512,512]{1,0:T(8,128)(2,1)} %pack.3), channel_id=1, source_target_pairs={{0,1},{1,0},{2,3},{3,2},{4,5},{5,4},{6,7},{7,6},{8,9},{9,8},{10,11... | collective-permute-start | bytes 1572872 | tf_op jit(solution)/shard_map/cond/branch_1_fun/ppermute | solution.py:758
  34.9 0.8 copy-start.3
  38.6 28.9 %all-to-all-start = ((bf16[16,64,512]{2,1,0:T(8,128)(2,1)}), bf16[16,64,512]{2,1,0:T(8,128)(2,1)S(1)}, u32[]{:S(2)}, u32[]{:S(2)}) async-start(bf16[16,64,512]{2,1,0:T(8,128)(2,1)} %bitcast.75), calls=%async_computation | async-start | bytes 2097152 | tf_op jit(solution)/shard_map/cond/branch_1_fun/all_to_all | solution.py:502
  43.3 26.7 %copy-start.5 = (bf16[512,1536]{1,0:T(8,128)(2,1)S(1)}, bf16[512,1536]{1,0:T(8,128)(2,1)}, u32[]{:S(2)}) copy-start(bf16[512,1536]{1,0:T(8,128)(2,1)} %get-tuple-element.74.weight_ref.key_weight_ref.value_weight_ref) | copy-start | bytes 4718596 | tf_op jit(solution)/shard_map/cond
  67.6 2.4 %copy-start.2 = (bf16[16,64,512]{2,1,0:T(8,128)(2,1)}, bf16[16,64,512]{2,1,0:T(8,128)(2,1)S(1)}, u32[]{:S(2)}) copy-start(bf16[16,64,512]{2,1,0:T(8,128)(2,1)S(1)} %all-to-all-done) | copy-start | bytes 3145732 | tf_op jit(solution)/shard_map/cond
  67.6 6.8 %collective-permute-start.1 = (bf16[1024,512]{1,0:T(8,128)(2,1)S(1)}, bf16[1024,512]{1,0:T(8,128)(2,1)S(1)}, u32[]{:S(2)}, u32[]{:S(2)}) collective-permute-start(bf16[1024,512]{1,0:T(8,128)(2,1)S(1)} %bitcast.81), channel_id=1, source_target_pairs={{0,1},{1,0},{2,3},{3,2},{4,5},{5,4},{6,7},{7,6},{8,9},{9,8},{10,11... | collective-permute-start | bytes 3145736 | tf_op jit(solution)/shard_map/cond/branch_1_fun/ppermute | solution.py:758
  74.3 1.0 copy-start.6
  98.5 33.8 %copy-start.13 = (bf16[2,512,512]{2,1,0:T(8,128)(2,1)S(1)}, bf16[2,512,512]{2,1,0:T(8,128)(2,1)}, u32[]{:S(2)}) copy-start(bf16[2,512,512]{2,1,0:T(8,128)(2,1)} %copy-done.12) | copy-start | bytes 3145732 | tf_op jit(solution)/shard_map/cond
  98.5 28.8 %all-to-all-start.1 = ((bf16[16,64,512]{2,1,0:T(8,128)(2,1)}), bf16[16,64,512]{2,1,0:T(8,128)(2,1)S(1)}, u32[]{:S(2)}, u32[]{:S(2)}) async-start(bf16[16,64,512]{2,1,0:T(8,128)(2,1)} %bitcast.84), calls=%async_computation.1 | async-start | bytes 2097152 | tf_op jit(solution)/shard_map/cond/branch_1_fun/all_to_all | solution.py:502
  127.4 4.1 %copy-start = (bf16[16,64,512]{2,1,0:T(8,128)(2,1)}, bf16[16,64,512]{2,1,0:T(8,128)(2,1)S(1)}, u32[]{:S(2)}) copy-start(bf16[16,64,512]{2,1,0:T(8,128)(2,1)S(1)} %all-to-all-done.1) | copy-start | bytes 3145732 | tf_op jit(solution)/shard_map/cond
  127.4 4.1 %collective-permute-start.2 = (bf16[512,512]{1,0:T(8,128)(2,1)S(1)}, bf16[512,512]{1,0:T(8,128)(2,1)S(1)}, u32[]{:S(2)}, u32[]{:S(2)}) collective-permute-start(bf16[512,512]{1,0:T(8,128)(2,1)S(1)} %bitcast.87), channel_id=1, source_target_pairs={{0,1},{1,0},{2,3},{3,2},{4,5},{5,4},{6,7},{7,6},{8,9},{9,8},{10,11... | collective-permute-start | bytes 1572872 | tf_op jit(solution)/shard_map/cond/branch_1_fun/ppermute | solution.py:758
  131.5 0.8 copy-start.9
